TPU v7x, 32 devices: a whole 2x2x4 slice. The times are simulated.
32 devices in a mesh: row: 4 (over y, x), col: 8 (over z, core).
Axes of the slice: x: 2, y: 2, z: 4, core: 2. Of those that a mesh axis runs over, the one named last changes fastest.
Arguments:
- local_ops: bfloat16 [4, 8, 2048, 2048], P('row', 'col'), may hold values from -2 to 30, as said below
- loads: float32 [4, 8, 2048, 256], P('row', 'col'), may hold values from -6 to 6
- modes: float32 [4, 8, 32, 2048], P('row', 'col'), may hold values from -1 to 1
- coarse_inverse: float32 [1024, 1024], P('row', 'col'), may hold values from -1 to 1
- face_rows: int32 [4, 8, 4, 512], P('row', 'col'), may hold values from 0 to 2047, as said below
- adjacency: int32 [4, 8, 4], P('row', 'col'), may hold values from 0 to 1, as said below
- contact: int32 [4, 8, 2048], P('row', 'col'), may hold values 0 or 1
Outputs:
- multipliers: float32 [4, 8, 2048, 256], P('row', 'col')
Inputs may be any that keep to these rules, and one draw needn't show every extreme that they name: `face_rows`: for each subdomain the 2048 entries are a permutation of 0 to 2047. `adjacency`: symmetric across each shared face (a subdomain's south flag equals the north flag of the one below it, its east flag the west flag of the one to its right); 0 on faces at the grid's edge. `local_ops`: each subdomain's local dual operator is symmetric positive definite.
All inputs are finite; a program needn't handle non-finite values. No bound on the sum of `contact` on one device may be relied on, other than what follows from the above.
Results may differ from a plain program's by a relative error of at most 0.00099.
Values sent between devices are 32-bit elements; how exact they have to be, the bound alone decides.
No kernel may reach another device: no remote copies, remote signals or barrier semaphores. Data moves between devices by JAX's collectives and lax.ppermute only.
A program may use at most 128 MiB of HBM per device.

v0:
```python
import jax
import jax.numpy as jnp
from jax import lax
from jax.sharding import PartitionSpec as P

ITERS = 2


def extended(block, sides, width):
    for axis, dim in sides:
        count = lax.axis_size(axis)
        forward = [(i, i + 1) for i in range(count - 1)]
        backward = [(target, source) for source, target in forward]
        low = lax.ppermute(
            lax.slice_in_dim(block, block.shape[dim] - width, None, axis=dim), axis, forward
        )
        high = lax.ppermute(lax.slice_in_dim(block, 0, width, axis=dim), axis, backward)
        block = jnp.concatenate([low, block, high], axis=dim)
    return block


def per_device(local_ops, loads, modes, coarse_inverse, face_rows, adjacency, contact):
    local_op = local_ops[0, 0]
    load_term = loads[0, 0]
    mode_rows = modes[0, 0]
    row_index = face_rows[0, 0]
    adj_flags = adjacency[0, 0].astype(jnp.float32)
    face_size = row_index.shape[1]
    order = load_term.shape[0]
    case_count = load_term.shape[1]
    flat_rows = row_index.reshape(-1)
    free_face = jnp.repeat(1.0 - adj_flags, face_size)
    row_free = jnp.zeros((order,), jnp.float32).at[flat_rows].set(free_face)
    weight = 0.5 + 0.5 * row_free
    clamp_rows = contact[0, 0].astype(jnp.float32) * row_free > 0.5

    def assemble(field_values):
        blocks = jnp.take(field_values, row_index, axis=0)
        vertical = extended(blocks[0:2], (("row", 0),), 1)
        lateral = extended(blocks[2:4], (("col", 0),), 1)
        incoming = (
            jnp.stack([vertical[0], vertical[3], lateral[0], lateral[3]]) * adj_flags[:, None, None]
        )
        return field_values.at[flat_rows].add(incoming.reshape(-1, case_count))

    multipliers = jnp.zeros((order, case_count), jnp.float32)
    for iteration in range(ITERS):
        if iteration == 0:
            local_term = -load_term
        else:
            local_term = (
                jnp.dot(
                    local_op, multipliers.astype(jnp.bfloat16), preferred_element_type=jnp.float32
                )
                - load_term
            )
        gradient = assemble(local_term)
        coarse_coef = jnp.dot(
            mode_rows, gradient, precision=lax.Precision.HIGHEST, preferred_element_type=jnp.float32
        )
        tile_cols = coarse_inverse.shape[1]
        col_index = lax.axis_index("col")
        gathered = lax.all_gather(coarse_coef, ("row", "col"), axis=0, tiled=True)
        coarse_block = lax.dynamic_slice_in_dim(gathered, col_index * tile_cols, tile_cols, 0)
        coarse_amount = lax.psum_scatter(
            jnp.dot(
                coarse_inverse,
                coarse_block,
                precision=lax.Precision.HIGHEST,
                preferred_element_type=jnp.float32,
            ),
            "col",
            scatter_dimension=0,
            tiled=True,
        )
        correction = lax.dot_general(
            mode_rows,
            coarse_amount,
            (((0,), (0,)), ((), ())),
            precision=lax.Precision.HIGHEST,
            preferred_element_type=jnp.float32,
        )
        direction = gradient - assemble(correction)
        direction_half = direction.astype(jnp.bfloat16)
        operated = jnp.dot(local_op, direction_half, preferred_element_type=jnp.float32)
        totals = lax.psum(
            (
                jnp.sum(weight[:, None] * direction * direction, axis=0),
                jnp.sum(direction * operated, axis=0),
            ),
            ("row", "col"),
        )
        step_length = totals[0] / totals[1]
        multipliers = multipliers - step_length[None, :] * direction
        multipliers = jnp.where(clamp_rows[:, None], jnp.maximum(multipliers, 0.0), multipliers)
    return multipliers[None, None]


def solution(mesh):
    placed = (
        P("row", "col", None, None),
        P("row", "col", None, None),
        P("row", "col", None, None),
        P("row", "col"),
        P("row", "col", None, None),
        P("row", "col", None),
        P("row", "col", None),
    )
    return jax.shard_map(
        per_device,
        mesh=mesh,
        in_specs=placed,
        out_specs=P("row", "col", None, None),
        check_vma=False,
    )
```

profile of v0, /device:TPU:0, one launch (start us, length us, event | category | flops | bytes accessed | tf_op | source)
XLA Modules:
  0.0 548.4 jit_solution(11973596477895200999)
XLA Ops:
  14.7 8.6 %gather_fusion = f32[2048,256]{1,0:T(8,128)} fusion(f32[2048,256]{1,0:T(8,128)S(1)} %copy.43, s32[2048]{0:T(1024)S(1)} %broadcast_clamp_fusion), kind=kCustom, calls=%fused_computation.clone | custom fusion | bytes 4202496 | tf_op jit(solution)/shard_map/jit(_take)/gather | solution.py:38
  25.4 4.9 collective-permute-start
  34.5 6.9 %collective-permute-done = f32[1,512,256]{2,1,0:T(8,128)S(1)} collective-permute-done((f32[1,512,256]{2,1,0:T(8,128)S(1)}, f32[1,512,256]{2,1,0:T(8,128)S(1)}, u32[]{:S(2)}, u32[]{:S(2)}) %collective-permute-start) | collective-permute-done | bytes 524320 | tf_op jit(solution)/shard_map/ppermute | solution.py:14
  41.4 13.2 %collective-permute-done.1 = f32[1,512,256]{2,1,0:T(8,128)S(1)} collective-permute-done((f32[1,512,256]{2,1,0:T(8,128)S(1)}, f32[1,512,256]{2,1,0:T(8,128)S(1)}, u32[]{:S(2)}, u32[]{:S(2)}) %collective-permute-start.1) | collective-permute-done | bytes 524320 | tf_op jit(solution)/shard_map/ppermute | solution.py:17
  56.4 12.7 %scatter_fusion = f32[2048,256]{1,0:T(8,128)S(1)} fusion(f32[2048,256]{1,0:T(8,128)S(1)} %copy.43, s32[2048]{0:T(1024)S(1)} %bitcast.114, f32[2048,256]{1,0:T(8,128)} %bitcast_multiply_fusion.3), kind=kCustom, calls=%fused_computation.5 | custom fusion | flops 524288 | bytes 6299648 | tf_op jit(solution)/shard_map/scatter-add | solution.py:44
  71.1 54.2 %all-gather.3.cloned.1.call-done = f32[1024,256]{1,0:T(8,128)} async-done(((f32[32,256]{1,0:T(8,128)}), f32[1024,256]{1,0:T(8,128)}) %all-gather.3.cloned.1.call-update) | async-done | bytes 1048592 | tf_op jit(solution)/shard_map/all_gather | solution.py:63
  127.5 29.4 %reduce-scatter.7.cloned.1.call-done = f32[32,256]{1,0:T(8,128)} async-done(((f32[256,256]{1,0:T(8,128)}), f32[32,256]{1,0:T(8,128)}) %reduce-scatter.7.cloned.1.call-update) | async-done | bytes 32784
  156.9 3.9 convolution_bitcast_fusion.1
  160.8 2.9 copy.45
  163.8 10.2 %gather_fusion.1 = f32[2048,256]{1,0:T(8,128)} fusion(f32[2048,256]{1,0:T(8,128)} %copy.45, s32[2048]{0:T(1024)S(1)} %broadcast_clamp_fusion), kind=kCustom, calls=%fused_computation.1.clone | custom fusion | bytes 4202496 | tf_op jit(solution)/shard_map/jit(_take)/gather | solution.py:38
  177.0 4.1 collective-permute-start.4
  186.0 8.0 %scatter_custom_fusion = f32[2048]{0:T(1024)S(1)} fusion(s32[2048]{0:T(1024)S(1)} %bitcast.115, f32[2048]{0:T(1024)S(1)} %bitcast.126, f32[]{:T(128)} %constant.16.clone.1), kind=kCustom, calls=%fused_computation.70 | custom fusion | bytes 8196 | tf_op jit(solution)/shard_map/scatter | solution.py:33
  195.9 6.0 %collective-permute-done.5 = f32[1,512,256]{2,1,0:T(8,128)} collective-permute-done((f32[1,512,256]{2,1,0:T(8,128)}, f32[1,512,256]{2,1,0:T(8,128)}, u32[]{:S(2)}, u32[]{:S(2)}) %collective-permute-start.5) | collective-permute-done | bytes 524320 | tf_op jit(solution)/shard_map/ppermute | solution.py:17
  205.8 13.2 %scatter_fusion.1 = f32[2048,256]{1,0:T(8,128)S(1)} fusion(f32[2048,256]{1,0:T(8,128)S(1)} %copy-done.1, s32[2048]{0:T(1024)S(1)} %bitcast.116, f32[2048,256]{1,0:T(8,128)} %bitcast_multiply_fusion.2), kind=kCustom, calls=%fused_computation.6 | custom fusion | flops 524288 | bytes 6299648 | tf_op jit(solution)/shard_map/scatter-add | solution.py:44
  223.5 6.7 %fusion.31 = f32[256]{0:T(256)S(1)} fusion(f32[2048,256]{0,1:T(8,128)S(1)} %get-tuple-element.13, bf16[1,1,2048,2048]{3,2,1,0:T(8,128)(2,1)} %param.9), kind=kOutput, calls=%fused_computation.41 | convolution fusion | flops 2149056256 | bytes 10486784 | tf_op jit(solution)/shard_map/dot_general | solution.py:85
  230.2 39.2 %all-reduce.1 = (f32[256]{0:T(256)S(1)}, f32[256]{0:T(256)S(1)}) all-reduce(f32[256]{0:T(256)S(1)} %get-tuple-element.12, f32[256]{0:T(256)S(1)} %fusion.31), channel_id=1, replica_groups=mesh['row'=4,'col'=8] {'row','col'}, use_global_device_ids=true, to_apply=%region_5.7 | all-reduce | flops 512 | bytes 4096 | tf_op jit(solution)/shard_map/psum | solution.py:86
  269.5 7.7 %fusion.21 = f32[2048,256]{0,1:T(8,128)} fusion(bf16[1,1,2048,2048]{3,2,1,0:T(8,128)(2,1)} %param.9, f32[1,1,2048,256]{2,3,1,0:T(8,128)S(1)} %copy-done.4, f32[2048,256]{0,1:T(8,128)} %copy-done.5, f32[256]{0:T(256)S(1)} %div.6, pred[2048]{0:T(1024)(128)(4,1)S(1)} %multiply_compare_fusion), kind=kOutput, calls=%fused_computation.26 | convolution fusion | flops 2150629376 | bytes 14683136 | tf_op jit(solution)/shard_map/dot_general | solution.py:52
  279.1 8.6 %gather_fusion.2 = f32[2048,256]{1,0:T(8,128)} fusion(f32[2048,256]{1,0:T(8,128)S(1)} %copy.49, s32[2048]{0:T(1024)S(1)} %broadcast_clamp_fusion), kind=kCustom, calls=%fused_computation.2.clone | custom fusion | bytes 4202496 | tf_op jit(solution)/shard_map/jit(_take)/gather | solution.py:38
  292.4 4.2 collective-permute-start.8
  298.0 8.4 %collective-permute-done.8 = f32[1,512,256]{2,1,0:T(8,128)S(1)} collective-permute-done((f32[1,512,256]{2,1,0:T(8,128)S(1)}, f32[1,512,256]{2,1,0:T(8,128)S(1)}, u32[]{:S(2)}, u32[]{:S(2)}) %collective-permute-start.8) | collective-permute-done | bytes 524320 | tf_op jit(solution)/shard_map/ppermute | solution.py:14
  306.4 13.1 %collective-permute-done.9 = f32[1,512,256]{2,1,0:T(8,128)S(1)} collective-permute-done((f32[1,512,256]{2,1,0:T(8,128)S(1)}, f32[1,512,256]{2,1,0:T(8,128)S(1)}, u32[]{:S(2)}, u32[]{:S(2)}) %collective-permute-start.9) | collective-permute-done | bytes 524320 | tf_op jit(solution)/shard_map/ppermute | solution.py:17
  321.3 12.9 %scatter_fusion.2 = f32[2048,256]{1,0:T(8,128)S(1)} fusion(f32[2048,256]{1,0:T(8,128)S(1)} %copy.49, s32[2048]{0:T(1024)S(1)} %bitcast.117, f32[2048,256]{1,0:T(8,128)} %bitcast_multiply_fusion.1), kind=kCustom, calls=%fused_computation.7 | custom fusion | flops 524288 | bytes 6299648 | tf_op jit(solution)/shard_map/scatter-add | solution.py:44
  336.1 57.0 %all-gather.5.cloned.1.call-done = f32[1024,256]{1,0:T(8,128)} async-done(((f32[32,256]{1,0:T(8,128)}), f32[1024,256]{1,0:T(8,128)}) %all-gather.5.cloned.1.call-update) | async-done | bytes 1048592 | tf_op jit(solution)/shard_map/all_gather | solution.py:63
  395.3 29.4 %reduce-scatter.9.cloned.1.call-done = f32[32,256]{1,0:T(8,128)} async-done(((f32[256,256]{1,0:T(8,128)}), f32[32,256]{1,0:T(8,128)}) %reduce-scatter.9.cloned.1.call-update) | async-done | bytes 32784
  424.8 3.9 convolution_bitcast_fusion
  431.6 10.2 %gather_fusion.3 = f32[2048,256]{1,0:T(8,128)} fusion(f32[2048,256]{1,0:T(8,128)} %copy.51, s32[2048]{0:T(1024)S(1)} %broadcast_clamp_fusion), kind=kCustom, calls=%fused_computation.3.clone | custom fusion | bytes 4202496 | tf_op jit(solution)/shard_map/jit(_take)/gather | solution.py:38
  444.9 3.4 collective-permute-start.12
  456.6 13.1 %collective-permute-done.13 = f32[1,512,256]{2,1,0:T(8,128)} collective-permute-done((f32[1,512,256]{2,1,0:T(8,128)}, f32[1,512,256]{2,1,0:T(8,128)}, u32[]{:S(2)}, u32[]{:S(2)}) %collective-permute-start.13) | collective-permute-done | bytes 524320 | tf_op jit(solution)/shard_map/ppermute | solution.py:17
  473.5 12.9 %scatter_fusion.3 = f32[2048,256]{1,0:T(8,128)S(1)} fusion(f32[2048,256]{1,0:T(8,128)S(1)} %copy-done.2, s32[2048]{0:T(1024)S(1)} %bitcast.118, f32[2048,256]{1,0:T(8,128)} %bitcast_multiply_fusion), kind=kCustom, calls=%fused_computation.8 | custom fusion | flops 524288 | bytes 6299648 | tf_op jit(solution)/shard_map/scatter-add | solution.py:44
  490.9 6.7 %fusion.28 = f32[256]{0:T(256)S(1)} fusion(f32[2048,256]{0,1:T(8,128)S(1)} %get-tuple-element.11, bf16[1,1,2048,2048]{3,2,1,0:T(8,128)(2,1)} %param.9), kind=kOutput, calls=%fused_computation.40 | convolution fusion | flops 2149056256 | bytes 10486784 | tf_op jit(solution)/shard_map/dot_general | solution.py:85
  497.6 39.2 %all-reduce = (f32[256]{0:T(256)S(1)}, f32[256]{0:T(256)S(1)}) all-reduce(f32[256]{0:T(256)S(1)} %get-tuple-element.10, f32[256]{0:T(256)S(1)} %fusion.28), channel_id=1, replica_groups=mesh['row'=4,'col'=8] {'row','col'}, use_global_device_ids=true, to_apply=%region_12.14 | all-reduce | flops 512 | bytes 4096 | tf_op jit(solution)/shard_map/psum | solution.py:86
  536.8 3.0 fusion.26
  (103 shorter events, 76.4 us)
Async XLA Ops:
  6.5 62.6 %copy-start = (f32[1,1,32,2048]{3,2,1,0:T(8,128)S(1)}, f32[1,1,32,2048]{3,2,1,0:T(8,128)}, u32[]{:S(2)}) copy-start(f32[1,1,32,2048]{3,2,1,0:T(8,128)} %param.11) | copy-start | bytes 786436
  6.5 118.7 %all-gather.3.cloned.1.call-start = ((), (), s32[]{:S(2)}) async-start(), calls=%async_computation.2 | async-start | bytes 1081344 | tf_op jit(solution)/shard_map/all_gather | solution.py:63
  9.9 1.3 copy-start.3
  25.2 9.2 %copy-start.10 = (s32[1,1,4]{2,1,0:T(1,128)S(1)}, s32[1,1,4]{2,1,0:T(1,128)}, u32[]{:S(2)}) copy-start(s32[1,1,4]{2,1,0:T(1,128)} %param.14) | copy-start | bytes 52
  25.2 9.2 %copy-start.8 = (s32[1,1,4,512]{3,2,1,0:T(4,128)S(1)}, s32[1,1,4,512]{3,2,1,0:T(4,128)}, u32[]{:S(2)}) copy-start(s32[1,1,4,512]{3,2,1,0:T(4,128)} %param.13) | copy-start | bytes 24580
  25.4 16.0 %collective-permute-start = (f32[1,512,256]{2,1,0:T(8,128)S(1)}, f32[1,512,256]{2,1,0:T(8,128)S(1)}, u32[]{:S(2)}, u32[]{:S(2)}) collective-permute-start(f32[1,512,256]{2,1,0:T(8,128)S(1)} %get-tuple-element.26), channel_id=1, source_target_pairs={{0,8},{8,16},{16,24},{1,9},{9,17},{17,25},{2,10},{10,18},{18,26},{... | collective-permute-start | bytes 1572872 | tf_op jit(solution)/shard_map/ppermute | solution.py:14
  30.3 24.3 %collective-permute-start.1 = (f32[1,512,256]{2,1,0:T(8,128)S(1)}, f32[1,512,256]{2,1,0:T(8,128)S(1)}, u32[]{:S(2)}, u32[]{:S(2)}) collective-permute-start(f32[1,512,256]{2,1,0:T(8,128)S(1)} %get-tuple-element.29), channel_id=1, source_target_pairs={{8,0},{16,8},{24,16},{9,1},{17,9},{25,17},{10,2},{18,10},{26,18},{... | collective-permute-start | bytes 1572872 | tf_op jit(solution)/shard_map/ppermute | solution.py:17
  31.6 23.0 %collective-permute-start.2 = (f32[1,512,256]{2,1,0:T(8,128)S(1)}, f32[1,512,256]{2,1,0:T(8,128)S(1)}, u32[]{:S(2)}, u32[]{:S(2)}) collective-permute-start(f32[1,512,256]{2,1,0:T(8,128)S(1)} %get-tuple-element.28), channel_id=1, source_target_pairs={{0,1},{1,2},{2,3},{3,4},{4,5},{5,6},{6,7},{8,9},{9,10},{10,11},{11... | collective-permute-start | bytes 1572872 | tf_op jit(solution)/shard_map/ppermute | solution.py:14
  33.1 21.5 %collective-permute-start.3 = (f32[1,512,256]{2,1,0:T(8,128)S(1)}, f32[1,512,256]{2,1,0:T(8,128)S(1)}, u32[]{:S(2)}, u32[]{:S(2)}) collective-permute-start(f32[1,512,256]{2,1,0:T(8,128)S(1)} %get-tuple-element.27), channel_id=1, source_target_pairs={{1,0},{2,1},{3,2},{4,3},{5,4},{6,5},{7,6},{9,8},{10,9},{11,10},{12... | collective-permute-start | bytes 1572872 | tf_op jit(solution)/shard_map/ppermute | solution.py:17
  69.2 56.1 %copy-start.7 = (f32[256,128]{1,0:T(8,128)S(1)}, f32[256,128]{1,0:T(8,128)}, u32[]{:S(2)}) copy-start(f32[256,128]{1,0:T(8,128)} %param.12) | copy-start | bytes 393220
  71.0 85.9 %reduce-scatter.7.cloned.1.call-start = ((), (), s32[]{:S(2)}) async-start(), calls=%async_computation.4 | async-start | bytes 294912
  127.4 265.7 %all-gather.5.cloned.1.call-start = ((), (), s32[]{:S(2)}) async-start(), calls=%async_computation.3 | async-start | bytes 1081344 | tf_op jit(solution)/shard_map/all_gather | solution.py:63
  175.8 10.1 %copy-start.9 = (s32[1,1,2048]{2,1,0:T(1,128)S(1)}, s32[1,1,2048]{2,1,0:T(1,128)}, u32[]{:S(2)}) copy-start(s32[1,1,2048]{2,1,0:T(1,128)} %param.15) | copy-start | bytes 24580
  177.0 18.9 %collective-permute-start.4 = (f32[1,512,256]{2,1,0:T(8,128)}, f32[1,512,256]{2,1,0:T(8,128)}, u32[]{:S(2)}, u32[]{:S(2)}) collective-permute-start(f32[1,512,256]{2,1,0:T(8,128)} %get-tuple-element.22), channel_id=1, source_target_pairs={{0,8},{8,16},{16,24},{1,9},{9,17},{17,25},{2,10},{10,18},{18,26},{... | collective-permute-start | bytes 1572872 | tf_op jit(solution)/shard_map/ppermute | solution.py:14
  181.2 20.7 %collective-permute-start.5 = (f32[1,512,256]{2,1,0:T(8,128)}, f32[1,512,256]{2,1,0:T(8,128)}, u32[]{:S(2)}, u32[]{:S(2)}) collective-permute-start(f32[1,512,256]{2,1,0:T(8,128)} %get-tuple-element.25), channel_id=1, source_target_pairs={{8,0},{16,8},{24,16},{9,1},{17,9},{25,17},{10,2},{18,10},{26,18},{... | collective-permute-start | bytes 1572872 | tf_op jit(solution)/shard_map/ppermute | solution.py:17
  182.5 19.4 %collective-permute-start.6 = (f32[1,512,256]{2,1,0:T(8,128)}, f32[1,512,256]{2,1,0:T(8,128)}, u32[]{:S(2)}, u32[]{:S(2)}) collective-permute-start(f32[1,512,256]{2,1,0:T(8,128)} %get-tuple-element.24), channel_id=1, source_target_pairs={{0,1},{1,2},{2,3},{3,4},{4,5},{5,6},{6,7},{8,9},{9,10},{10,11},{11... | collective-permute-start | bytes 1572872 | tf_op jit(solution)/shard_map/ppermute | solution.py:14
  184.6 17.3 %collective-permute-start.7 = (f32[1,512,256]{2,1,0:T(8,128)S(1)}, f32[1,512,256]{2,1,0:T(8,128)}, u32[]{:S(2)}, u32[]{:S(2)}) collective-permute-start(f32[1,512,256]{2,1,0:T(8,128)S(1)} %get-tuple-element.23), channel_id=1, source_target_pairs={{1,0},{2,1},{3,2},{4,3},{5,4},{6,5},{7,6},{9,8},{10,9},{11,10},{12... | collective-permute-start | bytes 1572872 | tf_op jit(solution)/shard_map/ppermute | solution.py:17
  203.5 2.3 copy-start.1
  223.5 6.7 %copy-start.5 = (f32[2048,256]{0,1:T(8,128)}, f32[2048,256]{0,1:T(8,128)S(1)}, u32[]{:S(2)}) copy-start(f32[2048,256]{0,1:T(8,128)S(1)} %get-tuple-element.13) | copy-start | bytes 6291460
  223.5 46.0 %copy-start.4 = (f32[1,1,2048,256]{2,3,1,0:T(8,128)S(1)}, f32[1,1,2048,256]{2,3,1,0:T(8,128)}, u32[]{:S(2)}) copy-start(f32[1,1,2048,256]{2,3,1,0:T(8,128)} %copy-done.3) | copy-start | bytes 6291460
  289.8 8.2 %collective-permute-start.10 = (f32[1,512,256]{2,1,0:T(8,128)S(1)}, f32[1,512,256]{2,1,0:T(8,128)S(1)}, u32[]{:S(2)}, u32[]{:S(2)}) collective-permute-start(f32[1,512,256]{2,1,0:T(8,128)S(1)} %get-tuple-element.20), channel_id=1, source_target_pairs={{0,1},{1,2},{2,3},{3,4},{4,5},{5,6},{6,7},{8,9},{9,10},{10,11},{11... | collective-permute-start | bytes 1572872 | tf_op jit(solution)/shard_map/ppermute | solution.py:14
  291.1 6.8 %collective-permute-start.11 = (f32[1,512,256]{2,1,0:T(8,128)S(1)}, f32[1,512,256]{2,1,0:T(8,128)S(1)}, u32[]{:S(2)}, u32[]{:S(2)}) collective-permute-start(f32[1,512,256]{2,1,0:T(8,128)S(1)} %get-tuple-element.19), channel_id=1, source_target_pairs={{1,0},{2,1},{3,2},{4,3},{5,4},{6,5},{7,6},{9,8},{10,9},{11,10},{12... | collective-permute-start | bytes 1572872 | tf_op jit(solution)/shard_map/ppermute | solution.py:17
  292.4 13.9 %collective-permute-start.8 = (f32[1,512,256]{2,1,0:T(8,128)S(1)}, f32[1,512,256]{2,1,0:T(8,128)S(1)}, u32[]{:S(2)}, u32[]{:S(2)}) collective-permute-start(f32[1,512,256]{2,1,0:T(8,128)S(1)} %get-tuple-element.18), channel_id=1, source_target_pairs={{0,8},{8,16},{16,24},{1,9},{9,17},{17,25},{2,10},{10,18},{18,26},{... | collective-permute-start | bytes 1572872 | tf_op jit(solution)/shard_map/ppermute | solution.py:14
  296.7 22.9 %collective-permute-start.9 = (f32[1,512,256]{2,1,0:T(8,128)S(1)}, f32[1,512,256]{2,1,0:T(8,128)S(1)}, u32[]{:S(2)}, u32[]{:S(2)}) collective-permute-start(f32[1,512,256]{2,1,0:T(8,128)S(1)} %get-tuple-element.21), channel_id=1, source_target_pairs={{8,0},{16,8},{24,16},{9,1},{17,9},{25,17},{10,2},{18,10},{26,18},{... | collective-permute-start | bytes 1572872 | tf_op jit(solution)/shard_map/ppermute | solution.py:17
  336.1 88.7 %reduce-scatter.9.cloned.1.call-start = ((), (), s32[]{:S(2)}) async-start(), calls=%async_computation.5 | async-start | bytes 294912
  444.9 11.7 %collective-permute-start.12 = (f32[1,512,256]{2,1,0:T(8,128)}, f32[1,512,256]{2,1,0:T(8,128)S(1)}, u32[]{:S(2)}, u32[]{:S(2)}) collective-permute-start(f32[1,512,256]{2,1,0:T(8,128)} %get-tuple-element.14), channel_id=1, source_target_pairs={{0,8},{8,16},{16,24},{1,9},{9,17},{17,25},{2,10},{10,18},{18,26},{... | collective-permute-start | bytes 1572872 | tf_op jit(solution)/shard_map/ppermute | solution.py:14
  448.3 21.4 %collective-permute-start.13 = (f32[1,512,256]{2,1,0:T(8,128)}, f32[1,512,256]{2,1,0:T(8,128)}, u32[]{:S(2)}, u32[]{:S(2)}) collective-permute-start(f32[1,512,256]{2,1,0:T(8,128)} %get-tuple-element.17), channel_id=1, source_target_pairs={{8,0},{16,8},{24,16},{9,1},{17,9},{25,17},{10,2},{18,10},{26,18},{... | collective-permute-start | bytes 1572872 | tf_op jit(solution)/shard_map/ppermute | solution.py:17
  449.6 20.1 %collective-permute-start.14 = (f32[1,512,256]{2,1,0:T(8,128)}, f32[1,512,256]{2,1,0:T(8,128)}, u32[]{:S(2)}, u32[]{:S(2)}) collective-permute-start(f32[1,512,256]{2,1,0:T(8,128)} %get-tuple-element.16), channel_id=1, source_target_pairs={{0,1},{1,2},{2,3},{3,4},{4,5},{5,6},{6,7},{8,9},{9,10},{10,11},{11... | collective-permute-start | bytes 1572872 | tf_op jit(solution)/shard_map/ppermute | solution.py:14
  451.7 18.0 %collective-permute-start.15 = (f32[1,512,256]{2,1,0:T(8,128)S(1)}, f32[1,512,256]{2,1,0:T(8,128)}, u32[]{:S(2)}, u32[]{:S(2)}) collective-permute-start(f32[1,512,256]{2,1,0:T(8,128)S(1)} %get-tuple-element.15), channel_id=1, source_target_pairs={{1,0},{2,1},{3,2},{4,3},{5,4},{6,5},{7,6},{9,8},{10,9},{11,10},{12... | collective-permute-start | bytes 1572872 | tf_op jit(solution)/shard_map/ppermute | solution.py:17
  471.2 2.3 copy-start.2
  490.9 6.7 %copy-start.6 = (f32[2048,256]{0,1:T(8,128)}, f32[2048,256]{0,1:T(8,128)S(1)}, u32[]{:S(2)}) copy-start(f32[2048,256]{0,1:T(8,128)S(1)} %get-tuple-element.11) | copy-start | bytes 6291460
Sparse Core Ops, SparseCore 0:
  71.1 54.0 all-gather.2
  127.5 29.3 reduce-scatter.6
  336.2 56.9 all-gather.4
  395.5 29.2 reduce-scatter.8
where the time goes:
time: 558 us; the launch traced here: 548 us
  waiting for transfers between devices  233 us (42%)
  other arithmetic  80.7 us (14%)
  blocking collectives  78.5 us (14%)
  local copies, waits for them, and re-layouts  73.4 us (13%)
  matrix products  35.2 us (6%)
  starting transfers between devices  34.1 us (6%)
  between operations  13.8 us (2%)
    all_gather x2, waiting for transfers between devices, per_device(): gathered = lax.all_gather(coarse_coef, ('row', 'col'), axis=0, tiled=True)  111 us
    psum x2, blocking collectives, per_device(): lax.psum((jnp.sum(weight[:, None] * direction * direction, axis=0), jnp.s...  78.5 us
    unnamed x6, waiting for transfers between devices  58.9 us
    scatter-add x4, other arithmetic, assemble(): return field_values.at[flat_rows].add(incoming.reshape(-1, case_count))  51.8 us
    ppermute x8, waiting for transfers between devices, extended(): lax.ppermute(lax.slice_in_dim(block, 0, width, axis=dim), axis, backward)  45.4 us
    gather x4, local copies, waits for them, and re-layouts, assemble(): blocks = jnp.take(field_values, row_index, axis=0)  37.5 us
    ppermute x8, starting transfers between devices, extended(): lax.ppermute(lax.slice_in_dim(block, block.shape[dim] - width, None, axis...  23.7 us
    ppermute x8, waiting for transfers between devices, extended(): lax.ppermute(lax.slice_in_dim(block, block.shape[dim] - width, None, axis...  17.1 us
  transfers between devices with their start and end apart: 20, of which 11 were waited for; matrix products, arithmetic and copies ran while one was open for 2% of the time, Pallas kernels for 0%

commit v1 on v0

v1 whole, which is shorter than its diff:
```python
import functools

import jax
import jax.numpy as jnp
from jax import lax
from jax.experimental import pallas as pl
from jax.experimental.pallas import tpu as pltpu
from jax.sharding import PartitionSpec as P

F32 = jnp.float32
BF16 = jnp.bfloat16
PAD = 8
MIB = 1024 * 1024
VMEM = pl.BlockSpec(memory_space=pltpu.VMEM)
SMEM = pl.BlockSpec(memory_space=pltpu.SMEM)
HBM = pl.BlockSpec(memory_space=pltpu.HBM)


def dot(a, b):
    return lax.dot_general(a, b, (((1,), (0,)), ((), ())), preferred_element_type=F32)


def dot_nt(a, b):
    return lax.dot_general(a, b, (((1,), (1,)), ((), ())), preferred_element_type=F32)


def parts_of(x):
    high = x.astype(BF16)
    return high, (x - high.astype(F32)).astype(BF16)


def dot3(a, b):
    return dot(a[0], b[0]) + (dot(a[0], b[1]) + dot(a[1], b[0]))


def column_of(row, lanes=128):
    return jnp.transpose(jnp.broadcast_to(row, (lanes, row.shape[1])))[:, :1]


def tile_rows(i, tile):
    return pl.ds(pl.multiple_of(i * tile, tile), tile)


def total_of(refs):
    value = refs[0][...]
    for ref in refs[1:]:
        value = value + ref[...]
    return value


def call(kernel, name, args, in_specs, outs, scratch, grant, flops):
    moved = sum(x.size * x.dtype.itemsize for x in args)
    return pl.pallas_call(
        kernel,
        in_specs=in_specs,
        out_specs=[VMEM] * len(outs),
        out_shape=outs,
        scratch_shapes=scratch,
        compiler_params=pltpu.CompilerParams(vmem_limit_bytes=grant * MIB),
        cost_estimate=pl.CostEstimate(flops=int(flops), bytes_accessed=int(moved), transcendentals=0),
        name=name,
    )(*args)


def in_hbm(x):
    return pltpu.with_memory_space_constraint(x, pltpu.HBM)


def in_vmem(arrays):
    return [pltpu.with_memory_space_constraint(x, pltpu.VMEM) for x in arrays]


def shaped(shape, dtype=F32):
    return pltpu.VMEM(shape, dtype)


def pair_face(base, index):
    return base + 1 - index % 2


def cross_face(base, index):
    return base + index % 2


def face_kernel(base, with_modes, place_ref, rows_ref, *refs):
    if base:
        x_parts, *refs = refs
        if with_modes:
            m_parts, *refs = refs
        outs = refs
    elif with_modes:
        sources, refs = refs[:2], refs[2:]
        *outs, x_parts, m_parts, x_ref, modes_ref, sems = refs
        copies = [
            pltpu.make_async_copy(source, held, sems.at[k])
            for k, (source, held) in enumerate(zip(sources, (x_ref, modes_ref)))
        ]
        for copy in copies:
            copy.start()
        for copy in copies:
            copy.wait()
        high, low = parts_of(modes_ref[...])
        count = modes_ref.shape[0]
        m_parts[:count] = high
        m_parts[count:] = low
    else:
        x_ref, *outs, x_parts = refs
    order, cases = x_parts.shape[0], x_parts.shape[1] // 2
    if not base:
        high, low = parts_of(x_ref[...])
        x_parts[:, :cases] = high
        x_parts[:, cases:] = low
    count = m_parts.shape[0] // 2 if with_modes else 0
    pair_ref, *cross_refs = outs
    index = place_ref[base // 2]
    half = rows_ref.shape[1] // 2
    chunks = half // cases
    lanes = lax.broadcasted_iota(jnp.int32, (half, order), 1)
    tall = half + chunks * count
    for k, face in enumerate((cross_face(base, index), pair_face(base, index))):
        for b in range(2):
            target, at = pair_ref, b * tall
            if k == 0:
                target, at = (cross_refs[0], at) if len(cross_refs) == 1 else (cross_refs[b], 0)
            column = column_of(rows_ref[pl.ds(face, 1), b * half : (b + 1) * half])
            picked = jnp.where(column == lanes, 1.0, 0.0).astype(BF16)
            got = dot(picked, x_parts[...])
            target[at : at + half] = got[:, :cases] + got[:, cases:]
            if with_modes:
                got = dot_nt(m_parts[...], picked)
                got = got[:count] + got[count:]
                for c in range(chunks):
                    begin = at + half + c * count
                    target[begin : begin + count] = got[:, c * cases : (c + 1) * cases]


def to_faces(base, place, rows, x, modes=None):
    order, cases = x.shape[0], x.shape[1] // (2 if base else 1)
    half = rows.shape[1] // 2
    tall = half
    args, scratch = [place, rows, x], []
    if modes is not None:
        count = modes.shape[0] // (2 if base else 1)
        tall += half // cases * count
        args = [place, rows, x, modes] if base else [place, rows, in_hbm(x), in_hbm(modes)]
        if not base:
            scratch = [pltpu.VMEM(arg.shape, arg.dtype) for arg in (x, modes)]
            scratch.append(pltpu.SemaphoreType.DMA((2,)))
    whole, part = shaped((2 * tall, cases)), shaped((tall, cases))
    outs = [whole, whole]
    if not base:
        outs = [whole, part, part, shaped((order, 2 * cases), BF16)]
        if modes is not None:
            outs.append(shaped((2 * count, order), BF16))
    return call(
        functools.partial(face_kernel, base, modes is not None),
        ("row" if base == 0 else "col") + "_faces",
        args,
        [SMEM, VMEM] + [HBM if scratch else VMEM] * (len(args) - 2),
        outs,
        scratch,
        8,
        2 * order * order * cases,
    )


def faces_of(kinds, place_ref):
    return [(cross_face if cross else pair_face)(base, place_ref[base // 2]) for base, cross in kinds]


def take_blocks(faces, adj_ref, blocks, half, count, r_parts):
    cases = blocks[0][0].shape[1]
    chunks = half // cases
    tall = half + chunks * count
    if count:
        r_parts[:, 2 * cases :] = jnp.zeros((r_parts.shape[0], r_parts.shape[1] - 2 * cases), BF16)
    for k, (face, block) in enumerate(zip(faces, blocks)):
        glued = adj_ref[face].astype(F32)
        for b in range(2):
            source, at = (block[b], 0) if len(block) == 2 else (block[0], b * tall)
            high, low = parts_of(source[at : at + half] * glued)
            begin = (2 * k + b) * half
            r_parts[begin : begin + half, :cases] = high
            r_parts[begin : begin + half, cases : 2 * cases] = low
            for c in range(chunks if count else 0):
                modes = at + half + c * count
                both = parts_of(jnp.transpose(source[modes : modes + count] * glued))
                rows = slice(begin + c * cases, begin + (c + 1) * cases)
                lane = 2 * cases + 2 * k * count
                r_parts[rows, lane : lane + 2 * count] = jnp.concatenate(both, axis=1)


def placed_rows(faces, rows_ref, begin, tile):
    ids = lax.broadcasted_iota(jnp.int32, (tile, rows_ref.shape[1]), 0) + begin
    return [jnp.where(rows_ref[pl.ds(face, 1), :] == ids, 1.0, 0.0) for face in faces]


def add_kernel(kinds, shape, last, tile, place_ref, adj_ref, rows_ref, x_ref, *refs):
    if last:
        modes_ref, sums_ref, *refs = refs
        *refs, out_ref, coef_ref, r_parts = refs
    else:
        *refs, out_ref, r_parts = refs
    order, cases = x_ref.shape
    faces = faces_of(kinds, place_ref)
    blocks = [[refs.pop(0) for _ in range(n)] for n in shape]
    take_blocks(faces, adj_ref, blocks, rows_ref.shape[1] // 2, 0, r_parts)

    @pl.loop(0, order // tile)
    def _(i):
        rows = tile_rows(i, tile)
        ones = placed_rows(faces, rows_ref, i * tile, tile)
        placed = jnp.concatenate([one.astype(BF16) for one in ones], axis=1)
        total = dot(placed, r_parts[...])
        out_ref[rows] = x_ref[rows] + (total[:, :cases] + total[:, cases:])

    if last:
        count = modes_ref.shape[0]
        coef_ref[:count] = dot3(parts_of(modes_ref[...]), parts_of(out_ref[...]))
        coef_ref[count:] = sums_ref[...]


def add_faces(kinds, place, adj, rows, x, blocks, ahead=None, tile=512):
    order, cases = x.shape
    args = [place, adj, rows, x] + list(ahead or []) + in_vmem(x for block in blocks for x in block)
    outs = [shaped((order, cases))]
    if ahead:
        outs.append(shaped((ahead[0].shape[0] + PAD, cases)))
    return call(
        functools.partial(add_kernel, kinds, [len(b) for b in blocks], bool(ahead), tile),
        "last_add" if ahead else "add",
        args,
        [SMEM, SMEM] + [VMEM] * (len(args) - 2),
        outs,
        [pltpu.VMEM((len(kinds) * rows.shape[1], 2 * cases), BF16)],
        6,
        len(kinds) * order * order * cases,
    )


def start_kernel(kinds, shape, last, count, tile, place_ref, adj_ref, rows_ref, x_ref, *refs):
    if last:
        glued_ref, near_ref, contact_ref, modes_ref, *refs = refs
        *refs, s_ref, w_high, w_low, weight_ref, clamp_ref, coef_ref, r_parts = refs
    else:
        op_ref, *refs = refs
        *refs, s_ref, near_ref, glued_ref, held, r_parts, sem = refs
        copy = pltpu.make_async_copy(op_ref, held, sem)
        copy.start()
    order, cases = x_ref.shape
    faces = faces_of(kinds, place_ref)
    blocks = [[refs.pop(0) for _ in range(n)] for n in shape]
    take_blocks(faces, adj_ref, blocks, rows_ref.shape[1] // 2, count, r_parts)

    @pl.loop(0, order // tile)
    def _(i):
        rows = tile_rows(i, tile)
        ones = placed_rows(faces, rows_ref, i * tile, tile)
        glued = jnp.zeros((tile, 1), F32)
        for face, one in zip(faces, ones):
            glued += adj_ref[face].astype(F32) * jnp.sum(one, axis=1, keepdims=True)
        total = dot(jnp.concatenate([one.astype(BF16) for one in ones], axis=1), r_parts[...])
        s = x_ref[rows] + (total[:, :cases] + total[:, cases : 2 * cases])
        near = []
        for k in range(len(faces)):
            lane = 2 * cases + 2 * k * count
            near.append(total[:, lane : lane + count] + total[:, lane + count : lane + 2 * count])
        if not last:
            s_ref[rows] = s
            near_ref[rows] = jnp.concatenate(near, axis=1)
            glued_ref[rows] = glued
        else:
            s_ref[rows] = -s
            row_free = 1.0 - (glued + glued_ref[rows])
            weight_ref[rows] = 0.5 + 0.5 * row_free
            contact = column_of(contact_ref[:, rows].astype(F32))
            clamp_ref[rows] = jnp.where(contact * row_free > 0.5, 1.0, 0.0)
            own = jnp.transpose(modes_ref[:, rows])
            high, low = parts_of(jnp.concatenate([own, near_ref[rows]] + near, axis=1))
            w_high[rows] = high
            w_low[rows] = low

    if last:
        coef_ref[...] = dot3(parts_of(modes_ref[...]), parts_of(s_ref[...]))
    else:
        copy.wait()


def start(kinds, place, adj, rows, x, blocks, count, op=None, ahead=None, tile=512):
    order, cases = x.shape
    column = shaped((order, 1))
    args = [place, adj, rows, x] + list(ahead or [in_hbm(op)]) + in_vmem(x for block in blocks for x in block)
    specs = [SMEM, SMEM, VMEM, VMEM] + [VMEM if ahead else HBM] + [VMEM] * (len(args) - 5)
    scratch = [pltpu.VMEM((len(kinds) * rows.shape[1], 2 * cases + 2 * len(kinds) * count), BF16)]
    if ahead:
        w = shaped((order, 5 * count), BF16)
        outs = [shaped((order, cases)), w, w, column, column, shaped((count, cases))]
    else:
        outs = [shaped((order, cases)), shaped((order, len(kinds) * count)), column, shaped(op.shape, op.dtype)]
        scratch.append(pltpu.SemaphoreType.DMA(()))
    return call(
        functools.partial(start_kernel, kinds, [len(b) for b in blocks], bool(ahead), count, tile),
        "last_start" if ahead else "start",
        args,
        specs,
        outs,
        scratch,
        10,
        len(kinds) * order * order * cases,
    )


def coarse_kernel(offsets, extra, grid_rows, place_ref, *refs):
    inverse_refs, refs = refs[:grid_rows], refs[grid_rows:]
    pieces = refs[: len(offsets)]
    outs = refs[len(offsets) : len(offsets) + grid_rows]
    coef, amounts = refs[len(offsets) + grid_rows :]
    row, col = place_ref[0], place_ref[1]
    count = inverse_refs[0].shape[1] // 3
    tall = count + extra
    sums = None
    for piece, inside in zip(pieces, offsets):
        for k, offset in enumerate(inside):
            begin = pl.multiple_of((col ^ offset) * count, count)
            coef[pl.ds(begin, count)] = piece[k * tall : k * tall + count]
            if extra:
                term = piece[k * tall + count : (k + 1) * tall]
                sums = term if sums is None else sums + term
    tiles = inverse_refs[0].shape[0]
    inverse = [jnp.concatenate([ref[k] for k in range(tiles)], axis=1) for ref in inverse_refs]
    inverse = parts_of(jnp.concatenate(inverse, axis=0))
    amounts[...] = dot3(inverse, parts_of(coef[...])).reshape(amounts.shape)
    odd = col % 2
    for j in range(grid_rows):
        target = row ^ j
        cross = jnp.clip(target - 1 + 2 * (target % 2), 0, grid_rows - 1) ^ row
        order = (j * 3 + 1, j * 3 + 2 - 2 * odd, j * 3 + 2 * odd, (j ^ 1) * 3 + 1, cross * 3 + 1)
        for k, source in enumerate(order):
            outs[j][k * count : (k + 1) * count] = amounts[source]
        if extra:
            outs[j][5 * count :] = sums


def coarse(place, inverse, pieces, offsets, extra):
    grid_rows = len(inverse)
    tiles, three, width = inverse[0].shape
    count = three // 3
    cases = pieces[0].shape[1]
    args = [place, *in_vmem(inverse), *in_vmem(pieces)]
    return call(
        functools.partial(coarse_kernel, offsets, extra, grid_rows),
        "coarse",
        args,
        [SMEM] + [VMEM] * (len(args) - 1),
        [shaped((5 * count + extra, cases))] * grid_rows,
        [pltpu.VMEM((tiles * width, cases), F32), pltpu.VMEM((grid_rows * 3, count, cases), F32)],
        4,
        6 * grid_rows * three * tiles * width * cases,
    )


def first_kernel(tile, op_ref, s_ref, w_high, w_low, clamp_ref, *refs):
    *part_refs, d_ref, v_ref, field = refs
    order, cases = s_ref.shape
    amount = parts_of(total_of(part_refs))

    @pl.loop(0, order // tile)
    def _(i):
        rows = tile_rows(i, tile)
        d = s_ref[rows] - dot3((w_high[rows], w_low[rows]), amount)
        d_ref[rows] = d
        h = jnp.where(clamp_ref[rows] > 0.5, jnp.maximum(-d, 0.0), -d)
        high, low = parts_of(h)
        field[rows, :cases] = high
        field[rows, cases:] = low

    @pl.loop(0, order // tile)
    def _(i):
        rows = tile_rows(i, tile)
        got = dot(op_ref[rows], field[...])
        v_ref[rows] = got[:, :cases] + got[:, cases:]


def first(op, s, w, clamp, amounts, tile=512):
    order, cases = s.shape
    args = [op, s, *w, clamp, *in_vmem(amounts)]
    return call(
        functools.partial(first_kernel, tile),
        "first",
        args,
        [VMEM] * len(args),
        [shaped((order, cases))] * 2,
        [pltpu.VMEM((order, 2 * cases), BF16)],
        6,
        4 * order * order * cases,
    )


def add_sums(sums_ref, tile, op_ref, d_ref, weight_ref, field):
    sums_ref[...] = jnp.zeros_like(sums_ref)

    @pl.loop(0, d_ref.shape[0] // tile)
    def _(i):
        rows = tile_rows(i, tile)
        operated = dot(op_ref[rows], field[...])
        d = d_ref[rows]
        sums_ref[0:1] += jnp.sum(weight_ref[rows] * d * d, axis=0, keepdims=True)
        sums_ref[1:2] += jnp.sum(d * operated, axis=0, keepdims=True)


def sums_kernel(tile, op_ref, d_ref, weight_ref, sums_ref, field):
    field[...] = d_ref[...].astype(BF16)
    add_sums(sums_ref, tile, op_ref, d_ref, weight_ref, field)


def step_sums(op, d, weight, tile=512):
    order, cases = d.shape
    return call(
        functools.partial(sums_kernel, tile),
        "step_sums",
        [op, d, weight],
        [VMEM] * 3,
        [shaped((PAD, cases))],
        [pltpu.VMEM((order, cases), BF16)],
        4,
        2 * order * order * cases,
    )[0]


def second_kernel(tile, op_ref, s_ref, d0_ref, w_high, w_low, weight_ref, *refs):
    *part_refs, d_ref, sums_ref, step_ref, field = refs
    order, cases = s_ref.shape
    wide = w_high.shape[1]
    amount = total_of(part_refs)
    length = amount[wide : wide + 1] / amount[wide + 1 : wide + 2]
    step_ref[...] = jnp.broadcast_to(length, step_ref.shape)
    amount = parts_of(amount[:wide])

    @pl.loop(0, order // tile)
    def _(i):
        rows = tile_rows(i, tile)
        q = s_ref[rows] - dot3((w_high[rows], w_low[rows]), amount)
        d = length * q + d0_ref[rows]
        d_ref[rows] = d
        field[rows] = d.astype(BF16)

    add_sums(sums_ref, tile, op_ref, d_ref, weight_ref, field)


def second(op, s, d0, w, weight, amounts, tile=512):
    order, cases = s.shape
    args = [op, s, d0, *w, weight, *in_vmem(amounts)]
    return call(
        functools.partial(second_kernel, tile),
        "second",
        args,
        [VMEM] * len(args),
        [shaped((order, cases)), shaped((PAD, cases)), shaped((PAD, cases))],
        [pltpu.VMEM((order, cases), BF16)],
        4,
        2 * order * order * cases,
    )


def finish_kernel(d0_ref, d1_ref, clamp_ref, step_ref, *refs):
    *sum_refs, out_ref = refs
    sums = total_of(sum_refs)
    low = jnp.where(clamp_ref[...] > 0.5, 0.0, -jnp.inf)
    once = jnp.maximum(-(step_ref[0:1] * d0_ref[...]), low)
    length = sums[0:1] / sums[1:2]
    out_ref[...] = jnp.maximum(once - length * d1_ref[...], low)


def finish(d0, d1, clamp, step, sums, tile=512):
    order, cases = d0.shape
    block = pl.BlockSpec((tile, cases), lambda i: (i, 0))
    small = pl.BlockSpec((PAD, cases), lambda i: (0, 0))
    return pl.pallas_call(
        finish_kernel,
        grid=(order // tile,),
        in_specs=[block, block, pl.BlockSpec((tile, 1), lambda i: (i, 0))] + [small] * (1 + len(sums)),
        out_specs=block,
        out_shape=jax.ShapeDtypeStruct((order, cases), F32),
        compiler_params=pltpu.CompilerParams(vmem_limit_bytes=16 * MIB),
        cost_estimate=pl.CostEstimate(flops=4 * order * cases, bytes_accessed=12 * order * cases, transcendentals=0),
        name="finish",
    )(d0, d1, clamp, step, *sums)


def send(x, axis, target):
    size = lax.axis_size(axis)
    pairs = [(i, target(i)) for i in range(size)]
    return lax.ppermute(x, axis, [(i, j) for i, j in pairs if j is not None and 0 <= j < size])


def swap(x, axis, bits):
    return send(x, axis, lambda i: i ^ bits)


def other_side(i):
    return i + 1 if i % 2 else i - 1


def row_exchange(pair, first_half, second_half):
    size = lax.axis_size("row")
    inside = lambda i: 0 <= other_side(i) < size
    one = send(first_half, "row", lambda i: i ^ 1 if inside(i) else None)
    two = send(second_half, "row", lambda i: (i + 2 if i % 2 else i - 2) if inside(i) else None)
    got = swap(pair, "row", 1)
    last = lambda: (
        send(one, "row", lambda i: (i - 2 if i % 2 else i + 2)),
        send(two, "row", lambda i: i ^ 1 if (0 <= (i - 2 if i % 2 else i + 2) < size) else None),
    )
    return got, (one, two), last


def col_exchange(pair, cross):
    return swap(pair, "col", 1), send(cross, "col", other_side)


def gather_cols(block):
    size = lax.axis_size("col")
    far = list(range(2, size, 2))
    pieces = [block] + [swap(block, "col", j) for j in far]
    held = jnp.concatenate(pieces, axis=0)
    known = [0] + far
    return pieces + [swap(held, "col", 1)], [[j] for j in known] + [[j ^ 1 for j in known]]


def coarse_amounts(place, inverse, block, extra):
    pieces, offsets = gather_cols(block)
    sends = coarse(place, inverse, pieces, offsets, extra)
    return [sends[0]] + [swap(sends[j], "row", j) for j in range(1, lax.axis_size("row"))]


def spread_cols(tile_block, count):
    grid_cols, tile_cols = lax.axis_size("col"), tile_block.shape[1]
    blocks = tile_block.reshape(grid_cols, count, tile_cols)
    three = jnp.concatenate([jnp.roll(blocks, 1, 0), blocks, jnp.roll(blocks, -1, 0)], axis=1)
    return three


def by_row(three):
    grid_rows = lax.axis_size("row")
    tiles = three.shape[0] // grid_rows
    row = lax.axis_index("row")
    return [lax.dynamic_slice_in_dim(three, (row ^ j) * tiles, tiles, 0) for j in range(grid_rows)]


def spread_rows(picked):
    return [picked[0]] + [swap(picked[j], "row", j) for j in range(1, len(picked))]


def after(x, *others):
    return lax.optimization_barrier((x, *others))[0]


EARLY = ((2, False), (2, True), (0, False))
LATE = ((0, True),)


def per_device(local_ops, loads, modes, coarse_inverse, face_rows, adjacency, contact):
    op, load, mode = local_ops[0, 0], loads[0, 0], modes[0, 0]
    rows, adj = face_rows[0, 0], adjacency[0, 0]
    touch = contact[0, 0][None]
    count = mode.shape[0]
    place = jnp.stack([lax.axis_index("row"), lax.axis_index("col")]).astype(jnp.int32)

    *row_sends, x_parts, m_parts = to_faces(0, place, rows, load, mode)
    pair, way, forward = row_exchange(*row_sends)
    three = spread_cols(after(coarse_inverse, row_sends[0]), count)
    col_sends = to_faces(2, after(place, three, *way), rows, x_parts, m_parts)
    three = lax.all_to_all(three, "col", 0, 0, tiled=True)
    col_got = col_exchange(*col_sends)
    blocks = [[col_got[0]], [col_got[1]], [pair]]
    part, near, glued, op = start(EARLY, place, adj, rows, load, blocks, count, op)
    picked = by_row(three)
    inverse = spread_rows(picked)
    s0, w_high, w_low, weight, clamp, coef = start(
        LATE, after(place, *picked), adj, rows, part, [forward()], count, None, [glued, near, touch, mode]
    )
    w = (w_high, w_low)
    amounts = coarse_amounts(place, inverse, coef, 0)
    d0, v = first(op, s0, w, clamp, amounts)

    *row_sends, x_parts = to_faces(0, place, rows, v)
    pair, way, forward = row_exchange(*row_sends)
    sums = step_sums(op, d0, after(weight, row_sends[0]))
    col_sends = to_faces(2, after(place, sums, *way), rows, x_parts)
    col_got = col_exchange(*col_sends)
    blocks = [[col_got[0]], [col_got[1]], [pair]]
    (part,) = add_faces(EARLY, place, adj, rows, v, blocks)
    s1, coef = add_faces(LATE, place, adj, rows, part, [forward()], [mode, sums])
    amounts = coarse_amounts(place, inverse, coef, PAD)
    d1, sums, step = second(op, s1, d0, w, weight, amounts)

    grid_rows, grid_cols = lax.axis_size("row"), lax.axis_size("col")
    sums = sum((swap(sums, "row", j) for j in range(1, grid_rows)), sums)
    sums = sum((swap(sums, "col", j) for j in range(2, grid_cols, 2)), sums)
    return finish(d0, d1, clamp, step, [sums, swap(sums, "col", 1)])[None, None]


def solution(mesh):
    placed = (
        P("row", "col", None, None),
        P("row", "col", None, None),
        P("row", "col", None, None),
        P("row", "col"),
        P("row", "col", None, None),
        P("row", "col", None),
        P("row", "col", None),
    )
    return jax.shard_map(
        per_device,
        mesh=mesh,
        in_specs=placed,
        out_specs=P("row", "col", None, None),
        check_vma=False,
    )
```

time: 558 us -> 168 us (0.30); the launches traced: 548 us -> 167 us
  waiting for transfers between devices: 233 us -> 40.9 us
  other arithmetic: 80.7 us -> 0.88 us
  blocking collectives: 78.5 us -> 0 us
  local copies, waits for them, and re-layouts: 73.4 us -> 4.71 us
  Pallas kernels: 0 us -> 57.3 us
  matrix products: 35.2 us -> 0 us
  starting transfers between devices: 34.1 us -> 63.2 us
  between operations: 13.8 us -> 0.37 us
    all_gather x2 -> x0, waiting for transfers between devices: 111 us -> none  [per_device(): gathered = lax.all_gather(coarse_coef, ('row', 'col'), axis=0, tiled=True)]
    psum x2 -> x0, blocking collectives: 78.5 us -> none  [per_device(): lax.psum((jnp.sum(weight[:, None] * direction * direction, axis=0), jnp.s...]
    unnamed x6 -> x0, waiting for transfers between devices: 58.9 us -> none
    pallas_call x0 -> x14, Pallas kernels: none -> 57.3 us  [the longest x13 55.2 us: call(): pl.pallas_call(kernel, in_specs=in_specs, out_specs=[VMEM] * len(outs), o...]
    scatter-add x4 -> x0, other arithmetic: 51.8 us -> none  [assemble(): return field_values.at[flat_rows].add(incoming.reshape(-1, case_count))]
    gather x4 -> x0, local copies, waits for them, and re-layouts: 37.5 us -> none  [assemble(): blocks = jnp.take(field_values, row_index, axis=0)]
    dot_general x9 -> x0, matrix products: 35.2 us -> none  [the longest x2 13.4 us: per_device(): jnp.dot(local_op, direction_half, preferred_element_type=jnp.float32)]
    ppermute x16 -> x38, starting transfers between devices: 34 us -> 56.9 us  [send(): lax.ppermute(x, axis, [(i, j) for i, j in pairs if j is not None and 0 <=...]
  transfers between devices with their start and end apart: 20 -> 39, of which waited for: 11 -> 20; matrix products, arithmetic and copies ran while one was open for 2% -> 1% of each run, Pallas kernels for 0% -> 15%
where the time goes in v1:
time: 168 us; the launch traced here: 167 us
  starting transfers between devices  63.2 us (38%)
  Pallas kernels  57.3 us (34%)
  waiting for transfers between devices  40.9 us (24%)
  local copies, waits for them, and re-layouts  4.71 us (3%)
    ppermute x38, starting transfers between devices, send(): lax.ppermute(x, axis, [(i, j) for i, j in pairs if j is not None and 0 <=...  56.9 us
    pallas_call x13, Pallas kernels, call(): pl.pallas_call(kernel, in_specs=in_specs, out_specs=[VMEM] * len(outs), o...  55.2 us
    ppermute x38, waiting for transfers between devices, send(): lax.ppermute(x, axis, [(i, j) for i, j in pairs if j is not None and 0 <=...  40.9 us
    all_to_all x1, starting transfers between devices, per_device(): three = lax.all_to_all(three, 'col', 0, 0, tiled=True)  6.33 us
    unnamed x18, local copies, waits for them, and re-layouts  3.63 us
  transfers between devices with their start and end apart: 39, of which 20 were waited for; matrix products, arithmetic and copies ran while one was open for 1% of the time, Pallas kernels for 15%

profile of v1, /device:TPU:0, one launch (start us, length us, event | category | flops | bytes accessed | tf_op | source)
XLA Modules:
  0.0 167.3 jit_solution(8842448121262406410)
XLA Ops:
  0.8 6.8 %row_faces.2 = (f32[576,256]{1,0:T(8,128)}, f32[288,256]{1,0:T(8,128)S(1)}, f32[288,256]{1,0:T(8,128)S(1)}, bf16[2048,512]{1,0:T(8,128)(2,1)S(1)}, bf16[64,2048]{1,0:T(8,128)(2,1)S(1)}) custom-call(s32[2]{0:T(128)S(1)} %pad_add_fusion.place_ref, s32[4,512]{1,0:T(4,128)S(1)} %bitcast.21, f32[2048,256]{1,0:T(8,128)} %bitcast.16, f32[32,2048]{1,0:T(8,128)} %bitcast.18), custom_call_target="tpu_custom_call" | custom-call | flops 2147483648 | bytes 2367496 | tf_op jit(solution)/shard_map/row_faces/pallas_call | solution.py:53
  12.5 6.3 %all-to-all-start = ((f32[8,96,128]{2,1,0:T(8,128)}), f32[8,96,128]{2,1,0:T(8,128)}, u32[]{:S(2)}, u32[]{:S(2)}) async-start(f32[8,96,128]{2,1,0:T(8,128)} %maximum_maximum_fusion), calls=%async_computation | async-start | bytes 786432 | tf_op jit(solution)/shard_map/all_to_all | solution.py:573
  18.8 4.4 %collective-permute-start.4 = (f32[576,256]{1,0:T(8,128)}, f32[576,256]{1,0:T(8,128)S(1)}, u32[]{:S(2)}, u32[]{:S(2)}) collective-permute-start(f32[576,256]{1,0:T(8,128)} %get-tuple-element.48), channel_id=1, source_target_pairs={{0,8},{8,0},{16,24},{24,16},{1,9},{9,1},{17,25},{25,17},{2,10},{10... | collective-permute-start | bytes 1769480 | tf_op jit(solution)/shard_map/ppermute | solution.py:493
  25.9 5.2 %col_faces.2 = (f32[576,256]{1,0:T(8,128)}, f32[576,256]{1,0:T(8,128)}) custom-call(s32[2]{0:T(128)S(1)} %pad_add_fusion.place_ref, s32[4,512]{1,0:T(4,128)S(1)} %bitcast.22, bf16[2048,512]{1,0:T(8,128)(2,1)S(1)} %copy-done.7, bf16[64,2048]{1,0:T(8,128)(2,1)S(1)} %get-tuple-element.54.refs_1_), custom_call_target="tpu_custom_call" | custom-call | flops 2147483648 | bytes 2367496 | tf_op jit(solution)/shard_map/col_faces/pallas_call | solution.py:53
  32.5 2.8 %collective-permute-start.5 = (f32[288,256]{1,0:T(8,128)}, f32[288,256]{1,0:T(8,128)}, u32[]{:S(2)}, u32[]{:S(2)}) collective-permute-start(f32[288,256]{1,0:T(8,128)} %collective-permute-done), channel_id=1, source_target_pairs={{0,16},{24,8},{1,17},{25,9},{2,18},{26,10},{3,19},{27,11},{4,20},{... | collective-permute-start | bytes 884744 | tf_op jit(solution)/shard_map/ppermute | solution.py:493
  35.3 2.0 %collective-permute-start.6 = (f32[288,256]{1,0:T(8,128)}, f32[288,256]{1,0:T(8,128)}, u32[]{:S(2)}, u32[]{:S(2)}) collective-permute-start(f32[288,256]{1,0:T(8,128)} %collective-permute-done.1), channel_id=1, source_target_pairs={{0,8},{24,16},{1,9},{25,17},{2,10},{26,18},{3,11},{27,19},{4,12},{... | collective-permute-start | bytes 884744 | tf_op jit(solution)/shard_map/ppermute | solution.py:493
  38.5 8.6 %start.1 = (f32[2048,256]{1,0:T(8,128)S(1)}, f32[2048,96]{1,0:T(8,128)S(1)}, f32[2048,1]{1,0:T(8,128)S(1)}, bf16[2048,2048]{1,0:T(8,128)(2,1)S(1)}) custom-call(s32[2]{0:T(128)S(1)} %pad_add_fusion.place_ref, s32[4]{0:T(128)S(1)} %bitcast.30, s32[4,512]{1,0:T(4,128)S(1)} %bitcast.23, f32[2048,256]{1,0:T(8,128)S(1)} %bitcast.17, bf16[2048,2048]{1,0:T(8,128)(2,1)} %bitcast.34, ...), custom_call_target="tpu_custom_call" | custom-call | flops 3221225472 | bytes 12263448 | tf_op jit(solution)/shard_map/start/pallas_call | solution.py:53
  47.1 4.7 %last_start.1 = (f32[2048,256]{1,0:T(8,128)S(1)}, bf16[2048,160]{1,0:T(8,128)(2,1)S(1)}, bf16[2048,160]{1,0:T(8,128)(2,1)S(1)}, f32[2048,1]{1,0:T(8,128)S(1)}, f...) custom-call(s32[2]{0:T(128)S(1)} %pad_add_fusion.place_ref, s32[4]{0:T(128)S(1)} %bitcast.31, s32[4,512]{1,0:T(4,128)S(1)} %bitcast.24, ...), custom_call_target="tpu_custom_call" | custom-call | flops 1073741824 | bytes 3760152 | tf_op jit(solution)/shard_map/last_start/pallas_call | solution.py:53
  51.8 7.8 %collective-permute-start.12 = (f32[32,256]{1,0:T(8,128)S(1)}, f32[32,256]{1,0:T(8,128)S(1)}, u32[]{:S(2)}, u32[]{:S(2)}) collective-permute-start(f32[32,256]{1,0:T(8,128)S(1)} %get-tuple-element.66.refs_4_), channel_id=1, source_target_pairs={{0,6},{1,7},{2,4},{3,5},{4,2},{5,3},{6,0},{7,1},{8,14},{9,15},{10,... | collective-permute-start | bytes 98312 | tf_op jit(solution)/shard_map/ppermute | solution.py:493
  61.7 2.7 %collective-permute-done.11.refs_6_ = f32[32,256]{1,0:T(8,128)S(1)} collective-permute-done((f32[32,256]{1,0:T(8,128)S(1)}, f32[32,256]{1,0:T(8,128)S(1)}, u32[]{:S(2)}, u32[]{:S(2)}) %collective-permute-start.11) | collective-permute-done | bytes 32800 | tf_op jit(solution)/shard_map/ppermute | solution.py:493
  65.9 2.2 %collective-permute-start.7 = (f32[2,96,128]{2,1,0:T(8,128)S(1)}, f32[2,96,128]{2,1,0:T(8,128)S(1)}, u32[]{:S(2)}, u32[]{:S(2)}) collective-permute-start(f32[2,96,128]{2,1,0:T(8,128)S(1)} %get-tuple-element.93), channel_id=1, source_target_pairs={{0,8},{8,0},{16,24},{24,16},{1,9},{9,1},{17,25},{25,17},{2,10},{10... | collective-permute-start | bytes 294920 | tf_op jit(solution)/shard_map/ppermute | solution.py:493
  68.1 3.0 %collective-permute-done.9.refs_3_ = f32[2,96,128]{2,1,0:T(8,128)S(1)} collective-permute-done((f32[2,96,128]{2,1,0:T(8,128)S(1)}, f32[2,96,128]{2,1,0:T(8,128)S(1)}, u32[]{:S(2)}, u32[]{:S(2)}) %collective-permute-start.9) | collective-permute-done | bytes 98336 | tf_op jit(solution)/shard_map/ppermute | solution.py:493
  77.2 3.6 %collective-permute-done.14.refs_1_ = f32[160,256]{1,0:T(8,128)S(1)} collective-permute-done((f32[160,256]{1,0:T(8,128)S(1)}, f32[160,256]{1,0:T(8,128)S(1)}, u32[]{:S(2)}, u32[]{:S(2)}) %collective-permute-start.14) | collective-permute-done | bytes 163872 | tf_op jit(solution)/shard_map/ppermute | solution.py:493
  80.8 2.7 %collective-permute-done.15.refs_2_ = f32[160,256]{1,0:T(8,128)S(1)} collective-permute-done((f32[160,256]{1,0:T(8,128)S(1)}, f32[160,256]{1,0:T(8,128)S(1)}, u32[]{:S(2)}, u32[]{:S(2)}) %collective-permute-start.15) | collective-permute-done | bytes 163872 | tf_op jit(solution)/shard_map/ppermute | solution.py:493
  83.5 6.6 %first.1 = (f32[2048,256]{1,0:T(8,128)S(1)}, f32[2048,256]{1,0:T(8,128)S(1)}) custom-call(bf16[2048,2048]{1,0:T(8,128)(2,1)S(1)} %get-tuple-element.57.op_ref, f32[2048,256]{1,0:T(8,128)S(1)} %get-tuple-element.62.s_ref, bf16[2048,160]{1,0:T(8,128)(2,1)S(1)} %get-tuple-element.63.w_high, bf16[2048,160]{1,0:T(8,128)(2,1)S(1)} %get-tuple-element.64.w_low, ...), custom_call_target="tpu_custom_call" | custom-call | flops 4294967296 | bytes 12460032 | tf_op jit(solution)/shard_map/first/pallas_call | solution.py:53
  90.1 3.2 %row_faces.3 = (f32[512,256]{1,0:T(8,128)S(1)}, f32[256,256]{1,0:T(8,128)S(1)}, f32[256,256]{1,0:T(8,128)S(1)}, bf16[2048,512]{1,0:T(8,128)(2,1)S(1)}) custom-call(s32[2]{0:T(128)S(1)} %pad_add_fusion.place_ref, s32[4,512]{1,0:T(4,128)S(1)} %bitcast.25, f32[2048,256]{1,0:T(8,128)S(1)} %get-tuple-element.72.refs_0_.x_ref), custom_call_target="tpu_custom_call" | custom-call | flops 2147483648 | bytes 2105352 | tf_op jit(solution)/shard_map/row_faces/pallas_call | solution.py:53
  95.9 2.7 %collective-permute-start.21 = (f32[512,256]{1,0:T(8,128)S(1)}, f32[512,256]{1,0:T(8,128)S(1)}, u32[]{:S(2)}, u32[]{:S(2)}) collective-permute-start(f32[512,256]{1,0:T(8,128)S(1)} %get-tuple-element.74), channel_id=1, source_target_pairs={{0,8},{8,0},{16,24},{24,16},{1,9},{9,1},{17,25},{25,17},{2,10},{10... | collective-permute-start | bytes 1572872 | tf_op jit(solution)/shard_map/ppermute | solution.py:493
  98.6 3.0 %step_sums.1.refs_1_ = f32[8,256]{1,0:T(8,128)S(1)} custom-call(bf16[2048,2048]{1,0:T(8,128)(2,1)S(1)} %get-tuple-element.57.op_ref, f32[2048,256]{1,0:T(8,128)S(1)} %get-tuple-element.71.d_ref.d0_ref, f32[2048,1]{1,0:T(8,128)S(1)} %get-tuple-element.75.weight_ref), custom_call_target="tpu_custom_call" | custom-call | flops 2147483648 | bytes 10493952 | tf_op jit(solution)/shard_map/step_sums/pallas_call | solution.py:53
  101.6 2.8 %collective-permute-done.17 = f32[256,256]{1,0:T(8,128)S(1)} collective-permute-done((f32[256,256]{1,0:T(8,128)S(1)}, f32[256,256]{1,0:T(8,128)S(1)}, u32[]{:S(2)}, u32[]{:S(2)}) %collective-permute-start.17) | collective-permute-done | bytes 262176 | tf_op jit(solution)/shard_map/ppermute | solution.py:493
  104.4 3.0 %col_faces.3 = (f32[512,256]{1,0:T(8,128)S(1)}, f32[512,256]{1,0:T(8,128)S(1)}) custom-call(s32[2]{0:T(128)S(1)} %pad_add_fusion.place_ref, s32[4,512]{1,0:T(4,128)S(1)} %bitcast.26, bf16[2048,512]{1,0:T(8,128)(2,1)S(1)} %get-tuple-element.79.refs_0_), custom_call_target="tpu_custom_call" | custom-call | flops 2147483648 | bytes 2105352 | tf_op jit(solution)/shard_map/col_faces/pallas_call | solution.py:53
  111.2 2.2 %collective-permute-done.21.refs_2_ = f32[512,256]{1,0:T(8,128)S(1)} collective-permute-done((f32[512,256]{1,0:T(8,128)S(1)}, f32[512,256]{1,0:T(8,128)S(1)}, u32[]{:S(2)}, u32[]{:S(2)}) %collective-permute-start.21) | collective-permute-done | bytes 524320 | tf_op jit(solution)/shard_map/ppermute | solution.py:493
  113.4 4.7 %add.49.x_ref = f32[2048,256]{1,0:T(8,128)S(1)} custom-call(s32[2]{0:T(128)S(1)} %pad_add_fusion.place_ref, s32[4]{0:T(128)S(1)} %bitcast.32, s32[4,512]{1,0:T(4,128)S(1)} %bitcast.27, f32[2048,256]{1,0:T(8,128)S(1)} %get-tuple-element.72.refs_0_.x_ref, f32[512,256]{1,0:T(8,128)S(1)} %collective-permute-done.19.refs_0_, ...), custom_call_target="tpu_custom_call" | custom-call | flops 3221225472 | bytes 3678232 | tf_op jit(solution)/shard_map/add/pallas_call | solution.py:53
  118.2 3.0 %last_add.1 = (f32[2048,256]{1,0:T(8,128)S(1)}, f32[40,256]{1,0:T(8,128)S(1)}) custom-call(s32[2]{0:T(128)S(1)} %pad_add_fusion.place_ref, s32[4]{0:T(128)S(1)} %bitcast.33, s32[4,512]{1,0:T(4,128)S(1)} %bitcast.28, f32[2048,256]{1,0:T(8,128)S(1)} %add.49.x_ref, f32[32,2048]{1,0:T(8,128)S(1)} %bitcast.20, f32[8,256]{1,0:T(8,128)S(1)} %step_sums.1.refs_1_, ...), custom_call_target="tpu_custom_call" | custom-call | flops 1073741824 | bytes 2899992 | tf_op jit(solution)/shard_map/last_add/pallas_call | solution.py:53
  121.2 6.5 %collective-permute-start.26 = (f32[40,256]{1,0:T(8,128)S(1)}, f32[40,256]{1,0:T(8,128)S(1)}, u32[]{:S(2)}, u32[]{:S(2)}) collective-permute-start(f32[40,256]{1,0:T(8,128)S(1)} %get-tuple-element.83.refs_4_), channel_id=1, source_target_pairs={{0,6},{1,7},{2,4},{3,5},{4,2},{5,3},{6,0},{7,1},{8,14},{9,15},{10,... | collective-permute-start | bytes 122888 | tf_op jit(solution)/shard_map/ppermute | solution.py:493
  129.8 3.2 %collective-permute-done.25.refs_6_ = f32[40,256]{1,0:T(8,128)S(1)} collective-permute-done((f32[40,256]{1,0:T(8,128)S(1)}, f32[40,256]{1,0:T(8,128)S(1)}, u32[]{:S(2)}, u32[]{:S(2)}) %collective-permute-start.25) | collective-permute-done | bytes 40992 | tf_op jit(solution)/shard_map/ppermute | solution.py:493
  135.6 1.9 %collective-permute-start.29 = (f32[168,256]{1,0:T(8,128)S(1)}, f32[168,256]{1,0:T(8,128)S(1)}, u32[]{:S(2)}, u32[]{:S(2)}) collective-permute-start(f32[168,256]{1,0:T(8,128)S(1)} %get-tuple-element.86), channel_id=1, source_target_pairs={{0,16},{8,24},{16,0},{24,8},{1,17},{9,25},{17,1},{25,9},{2,18},{10... | collective-permute-start | bytes 516104 | tf_op jit(solution)/shard_map/ppermute | solution.py:493
  139.0 3.7 %collective-permute-done.28.refs_1_ = f32[168,256]{1,0:T(8,128)S(1)} collective-permute-done((f32[168,256]{1,0:T(8,128)S(1)}, f32[168,256]{1,0:T(8,128)S(1)}, u32[]{:S(2)}, u32[]{:S(2)}) %collective-permute-start.28) | collective-permute-done | bytes 172064 | tf_op jit(solution)/shard_map/ppermute | solution.py:493
  142.8 3.0 %collective-permute-done.29.refs_2_ = f32[168,256]{1,0:T(8,128)S(1)} collective-permute-done((f32[168,256]{1,0:T(8,128)S(1)}, f32[168,256]{1,0:T(8,128)S(1)}, u32[]{:S(2)}, u32[]{:S(2)}) %collective-permute-start.29) | collective-permute-done | bytes 172064 | tf_op jit(solution)/shard_map/ppermute | solution.py:493
  145.7 4.4 %second.1 = (f32[2048,256]{1,0:T(8,128)S(1)}, f32[8,256]{1,0:T(8,128)S(1)}, f32[8,256]{1,0:T(8,128)S(1)}) custom-call(bf16[2048,2048]{1,0:T(8,128)(2,1)S(1)} %get-tuple-element.57.op_ref, f32[2048,256]{1,0:T(8,128)S(1)} %get-tuple-element.82.s_ref, f32[2048,256]{1,0:T(8,128)S(1)} %get-tuple-element.71.d_ref.d0_ref, ...), custom_call_target="tpu_custom_call" | custom-call | flops 2147483648 | bytes 14589952 | tf_op jit(solution)/shard_map/second/pallas_call | solution.py:53
  157.0 2.4 %collective-permute-start.36 = (f32[8,256]{1,0:T(8,128)S(1)}, f32[8,256]{1,0:T(8,128)S(1)}, u32[]{:S(2)}, u32[]{:S(2)}) collective-permute-start(f32[8,256]{1,0:T(8,128)S(1)} %add_add_fusion.1), channel_id=1, source_target_pairs={{0,6},{1,7},{2,4},{3,5},{4,2},{5,3},{6,0},{7,1},{8,14},{9,15},{10,... | collective-permute-start | bytes 24584 | tf_op jit(solution)/shard_map/ppermute | solution.py:493
  159.4 2.0 %collective-permute-start.34 = (f32[8,256]{1,0:T(8,128)S(1)}, f32[8,256]{1,0:T(8,128)S(1)}, u32[]{:S(2)}, u32[]{:S(2)}) collective-permute-start(f32[8,256]{1,0:T(8,128)S(1)} %add_add_fusion.1), channel_id=1, source_target_pairs={{0,2},{1,3},{2,0},{3,1},{4,6},{5,7},{6,4},{7,5},{8,10},{9,11},{10,... | collective-permute-start | bytes 24584 | tf_op jit(solution)/shard_map/ppermute | solution.py:493
  165.2 2.1 %finish.1 = f32[2048,256]{1,0:T(8,128)} custom-call(f32[2048,256]{1,0:T(8,128)S(1)} %get-tuple-element.71.d_ref.d0_ref, f32[2048,256]{1,0:T(8,128)S(1)} %get-tuple-element.88.d1_ref, f32[2048,1]{1,0:T(8,128)S(1)} %get-tuple-element.65.clamp_ref, f32[8,256]{1,0:T(8,128)S(1)} %get-tuple-element.89.step_ref, f32[8,256]{1,0:T(8,128)S(1)} %add_add_fusion.refs_0_, ...), custom_call_target="tpu_custom_call" | custom-call | flops 2097152 | bytes 6291456 | tf_op jit(solution)/shard_map/finish/pallas_call | solution.py:478
  (87 shorter events, 43.7 us)
Async XLA Ops:
  8.9 14.2 %collective-permute-start = (f32[288,256]{1,0:T(8,128)S(1)}, f32[288,256]{1,0:T(8,128)}, u32[]{:S(2)}, u32[]{:S(2)}) collective-permute-start(f32[288,256]{1,0:T(8,128)S(1)} %get-tuple-element.50), channel_id=1, source_target_pairs={{8,0},{16,24},{9,1},{17,25},{10,2},{18,26},{11,3},{19,27},{12,4},{... | collective-permute-start | bytes 884744 | tf_op jit(solution)/shard_map/ppermute | solution.py:493
  10.4 13.9 %collective-permute-start.1 = (f32[288,256]{1,0:T(8,128)S(1)}, f32[288,256]{1,0:T(8,128)}, u32[]{:S(2)}, u32[]{:S(2)}) collective-permute-start(f32[288,256]{1,0:T(8,128)S(1)} %get-tuple-element.51), channel_id=1, source_target_pairs={{8,24},{16,0},{9,25},{17,1},{10,26},{18,2},{11,27},{19,3},{12,28},... | collective-permute-start | bytes 884744 | tf_op jit(solution)/shard_map/ppermute | solution.py:493
  12.5 24.8 %all-to-all-start = ((f32[8,96,128]{2,1,0:T(8,128)}), f32[8,96,128]{2,1,0:T(8,128)}, u32[]{:S(2)}, u32[]{:S(2)}) async-start(f32[8,96,128]{2,1,0:T(8,128)} %maximum_maximum_fusion), calls=%async_computation | async-start | bytes 786432 | tf_op jit(solution)/shard_map/all_to_all | solution.py:573
  18.8 19.6 %collective-permute-start.4 = (f32[576,256]{1,0:T(8,128)}, f32[576,256]{1,0:T(8,128)S(1)}, u32[]{:S(2)}, u32[]{:S(2)}) collective-permute-start(f32[576,256]{1,0:T(8,128)} %get-tuple-element.48), channel_id=1, source_target_pairs={{0,8},{8,0},{16,24},{24,16},{1,9},{9,1},{17,25},{25,17},{2,10},{10... | collective-permute-start | bytes 1769480 | tf_op jit(solution)/shard_map/ppermute | solution.py:493
  31.1 7.3 %collective-permute-start.2 = (f32[576,256]{1,0:T(8,128)}, f32[576,256]{1,0:T(8,128)S(1)}, u32[]{:S(2)}, u32[]{:S(2)}) collective-permute-start(f32[576,256]{1,0:T(8,128)} %get-tuple-element.55), channel_id=1, source_target_pairs={{0,1},{1,0},{2,3},{3,2},{4,5},{5,4},{6,7},{7,6},{8,9},{9,8},{10,11... | collective-permute-start | bytes 1769480 | tf_op jit(solution)/shard_map/ppermute | solution.py:493
  31.1 7.3 %collective-permute-start.3 = (f32[576,256]{1,0:T(8,128)}, f32[576,256]{1,0:T(8,128)}, u32[]{:S(2)}, u32[]{:S(2)}) collective-permute-start(f32[576,256]{1,0:T(8,128)} %get-tuple-element.56), channel_id=1, source_target_pairs={{1,2},{2,1},{3,4},{4,3},{5,6},{6,5},{9,10},{10,9},{11,12},{12,11},... | collective-permute-start | bytes 1769480 | tf_op jit(solution)/shard_map/ppermute | solution.py:493
  32.5 14.5 %collective-permute-start.5 = (f32[288,256]{1,0:T(8,128)}, f32[288,256]{1,0:T(8,128)}, u32[]{:S(2)}, u32[]{:S(2)}) collective-permute-start(f32[288,256]{1,0:T(8,128)} %collective-permute-done), channel_id=1, source_target_pairs={{0,16},{24,8},{1,17},{25,9},{2,18},{26,10},{3,19},{27,11},{4,20},{... | collective-permute-start | bytes 884744 | tf_op jit(solution)/shard_map/ppermute | solution.py:493
  35.3 11.7 %collective-permute-start.6 = (f32[288,256]{1,0:T(8,128)}, f32[288,256]{1,0:T(8,128)}, u32[]{:S(2)}, u32[]{:S(2)}) collective-permute-start(f32[288,256]{1,0:T(8,128)} %collective-permute-done.1), channel_id=1, source_target_pairs={{0,8},{24,16},{1,9},{25,17},{2,10},{26,18},{3,11},{27,19},{4,12},{... | collective-permute-start | bytes 884744 | tf_op jit(solution)/shard_map/ppermute | solution.py:493
  51.8 9.9 %collective-permute-start.12 = (f32[32,256]{1,0:T(8,128)S(1)}, f32[32,256]{1,0:T(8,128)S(1)}, u32[]{:S(2)}, u32[]{:S(2)}) collective-permute-start(f32[32,256]{1,0:T(8,128)S(1)} %get-tuple-element.66.refs_4_), channel_id=1, source_target_pairs={{0,6},{1,7},{2,4},{3,5},{4,2},{5,3},{6,0},{7,1},{8,14},{9,15},{10,... | collective-permute-start | bytes 98312 | tf_op jit(solution)/shard_map/ppermute | solution.py:493
  59.6 4.8 %collective-permute-start.11 = (f32[32,256]{1,0:T(8,128)S(1)}, f32[32,256]{1,0:T(8,128)S(1)}, u32[]{:S(2)}, u32[]{:S(2)}) collective-permute-start(f32[32,256]{1,0:T(8,128)S(1)} %get-tuple-element.66.refs_4_), channel_id=1, source_target_pairs={{0,4},{1,5},{2,6},{3,7},{4,0},{5,1},{6,2},{7,3},{8,12},{9,13},{10,... | collective-permute-start | bytes 98312 | tf_op jit(solution)/shard_map/ppermute | solution.py:493
  59.6 4.8 %collective-permute-start.10 = (f32[32,256]{1,0:T(8,128)S(1)}, f32[32,256]{1,0:T(8,128)S(1)}, u32[]{:S(2)}, u32[]{:S(2)}) collective-permute-start(f32[32,256]{1,0:T(8,128)S(1)} %get-tuple-element.66.refs_4_), channel_id=1, source_target_pairs={{0,2},{1,3},{2,0},{3,1},{4,6},{5,7},{6,4},{7,5},{8,10},{9,11},{10,... | collective-permute-start | bytes 98312 | tf_op jit(solution)/shard_map/ppermute | solution.py:493
  64.4 8.3 %collective-permute-start.13 = (f32[128,256]{1,0:T(8,128)S(1)}, f32[128,256]{1,0:T(8,128)S(1)}, u32[]{:S(2)}, u32[]{:S(2)}) collective-permute-start(f32[128,256]{1,0:T(8,128)S(1)} %pad_maximum_fusion.1), channel_id=1, source_target_pairs={{0,1},{1,0},{2,3},{3,2},{4,5},{5,4},{6,7},{7,6},{8,9},{9,8},{10,11... | collective-permute-start | bytes 393224 | tf_op jit(solution)/shard_map/ppermute | solution.py:493
  64.5 6.6 %collective-permute-start.9 = (f32[2,96,128]{2,1,0:T(8,128)S(1)}, f32[2,96,128]{2,1,0:T(8,128)S(1)}, u32[]{:S(2)}, u32[]{:S(2)}) collective-permute-start(f32[2,96,128]{2,1,0:T(8,128)S(1)} %get-tuple-element.91), channel_id=1, source_target_pairs={{0,24},{8,16},{16,8},{24,0},{1,25},{9,17},{17,9},{25,1},{2,26},{10... | collective-permute-start | bytes 294920 | tf_op jit(solution)/shard_map/ppermute | solution.py:493
  65.9 6.8 %collective-permute-start.8 = (f32[2,96,128]{2,1,0:T(8,128)S(1)}, f32[2,96,128]{2,1,0:T(8,128)S(1)}, u32[]{:S(2)}, u32[]{:S(2)}) collective-permute-start(f32[2,96,128]{2,1,0:T(8,128)S(1)} %get-tuple-element.92), channel_id=1, source_target_pairs={{0,16},{8,24},{16,0},{24,8},{1,17},{9,25},{17,1},{25,9},{2,18},{10... | collective-permute-start | bytes 294920 | tf_op jit(solution)/shard_map/ppermute | solution.py:493
  65.9 6.8 %collective-permute-start.7 = (f32[2,96,128]{2,1,0:T(8,128)S(1)}, f32[2,96,128]{2,1,0:T(8,128)S(1)}, u32[]{:S(2)}, u32[]{:S(2)}) collective-permute-start(f32[2,96,128]{2,1,0:T(8,128)S(1)} %get-tuple-element.93), channel_id=1, source_target_pairs={{0,8},{8,0},{16,24},{24,16},{1,9},{9,1},{17,25},{25,17},{2,10},{10... | collective-permute-start | bytes 294920 | tf_op jit(solution)/shard_map/ppermute | solution.py:493
  73.7 7.1 %collective-permute-start.14 = (f32[160,256]{1,0:T(8,128)S(1)}, f32[160,256]{1,0:T(8,128)S(1)}, u32[]{:S(2)}, u32[]{:S(2)}) collective-permute-start(f32[160,256]{1,0:T(8,128)S(1)} %get-tuple-element.68), channel_id=1, source_target_pairs={{0,8},{8,0},{16,24},{24,16},{1,9},{9,1},{17,25},{25,17},{2,10},{10... | collective-permute-start | bytes 491528 | tf_op jit(solution)/shard_map/ppermute | solution.py:493
  74.1 9.3 %collective-permute-start.15 = (f32[160,256]{1,0:T(8,128)S(1)}, f32[160,256]{1,0:T(8,128)S(1)}, u32[]{:S(2)}, u32[]{:S(2)}) collective-permute-start(f32[160,256]{1,0:T(8,128)S(1)} %get-tuple-element.69), channel_id=1, source_target_pairs={{0,16},{8,24},{16,0},{24,8},{1,17},{9,25},{17,1},{25,9},{2,18},{10... | collective-permute-start | bytes 491528 | tf_op jit(solution)/shard_map/ppermute | solution.py:493
  75.6 7.9 %collective-permute-start.16 = (f32[160,256]{1,0:T(8,128)S(1)}, f32[160,256]{1,0:T(8,128)S(1)}, u32[]{:S(2)}, u32[]{:S(2)}) collective-permute-start(f32[160,256]{1,0:T(8,128)S(1)} %get-tuple-element.70), channel_id=1, source_target_pairs={{0,24},{8,16},{16,8},{24,0},{1,25},{9,17},{17,9},{25,1},{2,26},{10... | collective-permute-start | bytes 491528 | tf_op jit(solution)/shard_map/ppermute | solution.py:493
  93.3 11.1 %collective-permute-start.17 = (f32[256,256]{1,0:T(8,128)S(1)}, f32[256,256]{1,0:T(8,128)S(1)}, u32[]{:S(2)}, u32[]{:S(2)}) collective-permute-start(f32[256,256]{1,0:T(8,128)S(1)} %get-tuple-element.76), channel_id=1, source_target_pairs={{8,0},{16,24},{9,1},{17,25},{10,2},{18,26},{11,3},{19,27},{12,4},{... | collective-permute-start | bytes 786440 | tf_op jit(solution)/shard_map/ppermute | solution.py:493
  94.6 9.8 %collective-permute-start.18 = (f32[256,256]{1,0:T(8,128)S(1)}, f32[256,256]{1,0:T(8,128)S(1)}, u32[]{:S(2)}, u32[]{:S(2)}) collective-permute-start(f32[256,256]{1,0:T(8,128)S(1)} %get-tuple-element.77), channel_id=1, source_target_pairs={{8,24},{16,0},{9,25},{17,1},{10,26},{18,2},{11,27},{19,3},{12,28},... | collective-permute-start | bytes 786440 | tf_op jit(solution)/shard_map/ppermute | solution.py:493
  95.9 17.5 %collective-permute-start.21 = (f32[512,256]{1,0:T(8,128)S(1)}, f32[512,256]{1,0:T(8,128)S(1)}, u32[]{:S(2)}, u32[]{:S(2)}) collective-permute-start(f32[512,256]{1,0:T(8,128)S(1)} %get-tuple-element.74), channel_id=1, source_target_pairs={{0,8},{8,0},{16,24},{24,16},{1,9},{9,1},{17,25},{25,17},{2,10},{10... | collective-permute-start | bytes 1572872 | tf_op jit(solution)/shard_map/ppermute | solution.py:493
  107.4 6.0 %collective-permute-start.19 = (f32[512,256]{1,0:T(8,128)S(1)}, f32[512,256]{1,0:T(8,128)S(1)}, u32[]{:S(2)}, u32[]{:S(2)}) collective-permute-start(f32[512,256]{1,0:T(8,128)S(1)} %get-tuple-element.80), channel_id=1, source_target_pairs={{0,1},{1,0},{2,3},{3,2},{4,5},{5,4},{6,7},{7,6},{8,9},{9,8},{10,11... | collective-permute-start | bytes 1572872 | tf_op jit(solution)/shard_map/ppermute | solution.py:493
  107.5 5.9 %collective-permute-start.20 = (f32[512,256]{1,0:T(8,128)S(1)}, f32[512,256]{1,0:T(8,128)S(1)}, u32[]{:S(2)}, u32[]{:S(2)}) collective-permute-start(f32[512,256]{1,0:T(8,128)S(1)} %get-tuple-element.81), channel_id=1, source_target_pairs={{1,2},{2,1},{3,4},{4,3},{5,6},{6,5},{9,10},{10,9},{11,12},{12,11},... | collective-permute-start | bytes 1572872 | tf_op jit(solution)/shard_map/ppermute | solution.py:493
  108.2 9.9 %collective-permute-start.22 = (f32[256,256]{1,0:T(8,128)S(1)}, f32[256,256]{1,0:T(8,128)S(1)}, u32[]{:S(2)}, u32[]{:S(2)}) collective-permute-start(f32[256,256]{1,0:T(8,128)S(1)} %collective-permute-done.17), channel_id=1, source_target_pairs={{0,16},{24,8},{1,17},{25,9},{2,18},{26,10},{3,19},{27,11},{4,20},{... | collective-permute-start | bytes 786440 | tf_op jit(solution)/shard_map/ppermute | solution.py:493
  109.6 8.5 %collective-permute-start.23 = (f32[256,256]{1,0:T(8,128)S(1)}, f32[256,256]{1,0:T(8,128)S(1)}, u32[]{:S(2)}, u32[]{:S(2)}) collective-permute-start(f32[256,256]{1,0:T(8,128)S(1)} %collective-permute-done.18), channel_id=1, source_target_pairs={{0,8},{24,16},{1,9},{25,17},{2,10},{26,18},{3,11},{27,19},{4,12},{... | collective-permute-start | bytes 786440 | tf_op jit(solution)/shard_map/ppermute | solution.py:493
  121.2 8.6 %collective-permute-start.26 = (f32[40,256]{1,0:T(8,128)S(1)}, f32[40,256]{1,0:T(8,128)S(1)}, u32[]{:S(2)}, u32[]{:S(2)}) collective-permute-start(f32[40,256]{1,0:T(8,128)S(1)} %get-tuple-element.83.refs_4_), channel_id=1, source_target_pairs={{0,6},{1,7},{2,4},{3,5},{4,2},{5,3},{6,0},{7,1},{8,14},{9,15},{10,... | collective-permute-start | bytes 122888 | tf_op jit(solution)/shard_map/ppermute | solution.py:493
  127.7 5.3 %collective-permute-start.25 = (f32[40,256]{1,0:T(8,128)S(1)}, f32[40,256]{1,0:T(8,128)S(1)}, u32[]{:S(2)}, u32[]{:S(2)}) collective-permute-start(f32[40,256]{1,0:T(8,128)S(1)} %get-tuple-element.83.refs_4_), channel_id=1, source_target_pairs={{0,4},{1,5},{2,6},{3,7},{4,0},{5,1},{6,2},{7,3},{8,12},{9,13},{10,... | collective-permute-start | bytes 122888 | tf_op jit(solution)/shard_map/ppermute | solution.py:493
  128.0 5.1 %collective-permute-start.24 = (f32[40,256]{1,0:T(8,128)S(1)}, f32[40,256]{1,0:T(8,128)S(1)}, u32[]{:S(2)}, u32[]{:S(2)}) collective-permute-start(f32[40,256]{1,0:T(8,128)S(1)} %get-tuple-element.83.refs_4_), channel_id=1, source_target_pairs={{0,2},{1,3},{2,0},{3,1},{4,6},{5,7},{6,4},{7,5},{8,10},{9,11},{10,... | collective-permute-start | bytes 122888 | tf_op jit(solution)/shard_map/ppermute | solution.py:493
  135.5 7.3 %collective-permute-start.28 = (f32[168,256]{1,0:T(8,128)S(1)}, f32[168,256]{1,0:T(8,128)S(1)}, u32[]{:S(2)}, u32[]{:S(2)}) collective-permute-start(f32[168,256]{1,0:T(8,128)S(1)} %get-tuple-element.85), channel_id=1, source_target_pairs={{0,8},{8,0},{16,24},{24,16},{1,9},{9,1},{17,25},{25,17},{2,10},{10... | collective-permute-start | bytes 516104 | tf_op jit(solution)/shard_map/ppermute | solution.py:493
  135.6 10.2 %collective-permute-start.29 = (f32[168,256]{1,0:T(8,128)S(1)}, f32[168,256]{1,0:T(8,128)S(1)}, u32[]{:S(2)}, u32[]{:S(2)}) collective-permute-start(f32[168,256]{1,0:T(8,128)S(1)} %get-tuple-element.86), channel_id=1, source_target_pairs={{0,16},{8,24},{16,0},{24,8},{1,17},{9,25},{17,1},{25,9},{2,18},{10... | collective-permute-start | bytes 516104 | tf_op jit(solution)/shard_map/ppermute | solution.py:493
  137.5 8.2 %collective-permute-start.30 = (f32[168,256]{1,0:T(8,128)S(1)}, f32[168,256]{1,0:T(8,128)S(1)}, u32[]{:S(2)}, u32[]{:S(2)}) collective-permute-start(f32[168,256]{1,0:T(8,128)S(1)} %get-tuple-element.87), channel_id=1, source_target_pairs={{0,24},{8,16},{16,8},{24,0},{1,25},{9,17},{17,9},{25,1},{2,26},{10... | collective-permute-start | bytes 516104 | tf_op jit(solution)/shard_map/ppermute | solution.py:493
  157.0 5.4 %collective-permute-start.36 = (f32[8,256]{1,0:T(8,128)S(1)}, f32[8,256]{1,0:T(8,128)S(1)}, u32[]{:S(2)}, u32[]{:S(2)}) collective-permute-start(f32[8,256]{1,0:T(8,128)S(1)} %add_add_fusion.1), channel_id=1, source_target_pairs={{0,6},{1,7},{2,4},{3,5},{4,2},{5,3},{6,0},{7,1},{8,14},{9,15},{10,... | collective-permute-start | bytes 24584 | tf_op jit(solution)/shard_map/ppermute | solution.py:493
  (16 other events, 95.9 us)
